TPU v7x, 512 devices: a whole 4x8x8 slice. The times are simulated.
512 devices in a mesh: grp: 4 (over x), seq: 32 (over y_lo, z, core), tp: 4 (over y_hi).
Axes of the slice: x: 4, y: 8 (y_hi: 4, y_lo: 2; y = y_hi * 2 + y_lo), z: 8, core: 2. Of those that a mesh axis runs over, the one named last changes fastest.
Arguments:
- latent: bfloat16 [8192, 3072], P('seq'), may hold values from -6 to 6
- condition: bfloat16 [8192, 3072], P('seq'), may hold values from -6 to 6
- modulation: float32 [2, 3, 3072], replicated, may hold values from -3 to 3
- qk_gain: float32 [2, 2, 128], replicated, may hold values from 1.2 to 2.4
- qkv_weight: bfloat16 [2, 3, 3072, 2048], P(None, None, 'seq', ('grp', 'tp')), may hold values from -0.109375 to 0.109375
- out_weight: bfloat16 [2, 2048, 3072], P(None, ('grp', 'tp'), 'seq'), may hold values from -0.25 to 0.25
Outputs:
- mixed: bfloat16 [8192, 3072], P('seq', ('grp', 'tp'))
All inputs are finite; a program needn't handle non-finite values.
Results may differ from a plain program's by a relative error of at most 0.015.
Values may be sent and summed in bfloat16 or wider, within the bound.
A program may use at most 128 MiB of HBM per device.

v0:
```python
import math

import jax
import jax.numpy as jnp
from jax import lax
from jax.experimental import pallas as pl
from jax.experimental.pallas import tpu as pltpu
from jax.sharding import PartitionSpec as P

MESH = pl.DeviceIdType.MESH
BF16, F32 = jnp.bfloat16, jnp.float32
Z = 8
ROWS = 256
CHIP = 2 * ROWS
D = 3072
HEAD = 128
WROWS = 96
N_SEMS = 200


def kernel(
    lat_in, cond_in, mod_in, gain, wsh, ow_in, out,
    lat, cond, mod, ow, owt, wbuf, xbuf, xst, qbuf, kbuf, vbuf, kst, vst, qst, owb, acc, abuf, ast, pst, rbuf, res,
    send_sems, recv_sems, load_sems,
):
    loads = []
    for i, (a, b) in enumerate(((ow_in, ow), (mod_in, mod), (lat_in, lat), (cond_in, cond))):
        loads.append(pltpu.make_async_copy(a, b, load_sems.at[i]))
        loads[-1].start()
    x, s, tp = lax.axis_index("grp"), lax.axis_index("seq"), lax.axis_index("tp")
    y, z, c = s // 16, (s // 2) % 8, s % 2

    def seq_of(y_, z_, c_):
        return y_ * 16 + z_ * 2 + c_

    sib = {"seq": seq_of(y, z, 1 - c)}
    row = {"seq": seq_of(1 - y, z, c)}
    diag = {"seq": seq_of(1 - y, z, 1 - c)}
    right = {"seq": seq_of(y, (z + 1) % Z, c)}
    left = {"seq": seq_of(y, (z + 7) % Z, c)}

    def zm(t):
        return (z + Z - t) % Z

    def zp(t):
        return (z + t) % Z

    px, py, pz = y * 2 + z // 4, x // 2, z % 4 + 4 * (x % 2)
    moves = px != x
    partner = {"grp": px, "seq": seq_of(py, pz, c)}

    barrier = pltpu.get_barrier_semaphore()

    def greet(device):
        pl.semaphore_signal(barrier, inc=1, device_id=device, device_id_type=MESH)

    flat = x * 4 + y * 2 + c
    for i in range(1, 16):
        f = (flat + i) % 16
        greet({"grp": f // 4, "seq": seq_of((f // 2) % 2, z, f % 2)})
    for dz in (1, 7):
        for core in (c, 1 - c):
            greet({"seq": seq_of(y, (z + dz) % Z, core)})
    for i in range(1, 4):
        greet({"tp": (tp + i) % 4})

    @pl.when(moves)
    def _():
        greet(partner)

    pl.semaphore_wait(barrier, 22 + jnp.where(moves, 1, 0))

    ids = iter(range(N_SEMS))
    sent = []

    def remote(src, dst, device, i):
        return pltpu.make_async_remote_copy(
            src_ref=src, dst_ref=dst, send_sem=send_sems.at[i], recv_sem=recv_sems.at[i],
            device_id=device, device_id_type=MESH,
        )

    def push(src, dst, device):
        i = next(ids)
        copy = remote(src, dst, device, i)
        copy.start()
        sent.append(copy)
        return i

    def arrived(land, i):
        remote(land, land, sib, i).wait_recv()

    def ring_send(view, t):
        if t < 3:
            a, b = view(zm(t), None), view(zp(t), None)
        else:
            a, b = view(zm(t), 0), view(zp(t), 1)
        return push(a, a, right), push(b, b, left)

    def ring_wait(view, t, got):
        if t < 4:
            arrived(view(zm(t), None), got[0])
            arrived(view(zp(t), None), got[1])
        else:
            arrived(view(zm(t), 0), got[0])
            arrived(view(zp(t), 1), got[1])

    own_rows = pl.ds(pl.multiple_of(c * WROWS, 32), WROWS)
    sib_rows = pl.ds(pl.multiple_of((1 - c) * WROWS, 32), WROWS)
    k_first, y_first = {}, []
    for e, core in enumerate((c, 1 - c)):
        for dz in (1, 7):
            near_by = {"seq": seq_of(y, (z + dz) % Z, core)}
            k_first[dz, e] = push(wsh.at[core, 1], wbuf.at[1, y, z, own_rows], near_by)
        across = {"seq": seq_of(1 - y, z, core)}
        y_first.append(push(wsh.at[core, 1:3], wbuf.at[1:3, y, z, own_rows], across))
    w_sib = push(wsh.at[1 - c], wbuf.at[:, y, z, own_rows], sib)
    w_own = pltpu.make_async_copy(wsh.at[c], wbuf.at[:, y, z, own_rows], load_sems.at[4])
    w_own.start()

    ow_id = next(ids)
    ow_copy = remote(owt, owb.at[seq_of(py, pz, c)], partner, ow_id)
    loads[0].wait()
    loads[1].wait()
    first = s * WROWS
    base = jnp.minimum(first // HEAD * HEAD, D - 2 * HEAD)
    for block in range(2):
        gates = mod[2, block:block + 1, pl.ds(pl.multiple_of(base, HEAD), 2 * HEAD)]
        gates = pltpu.roll(jnp.broadcast_to(gates, (HEAD, 2 * HEAD)), (2 * HEAD + base - first) % (2 * HEAD), 1)
        gates = jnp.transpose(gates[:, :WROWS])
        owt[:, block * HEAD:(block + 1) * HEAD] = (ow[block].astype(F32) * gates).astype(BF16)

    @pl.when(moves)
    def _():
        ow_copy.start()

    @pl.when(jnp.logical_not(moves))
    def _():
        owb[s] = owt[...]

    def layer_norm(block, store, lo, hi):
        use = jnp.where(block == 0, 1.0, 0.0).astype(F32)
        scale = 1.0 + mod[1, pl.ds(block, 1), :]
        shift = mod[0, pl.ds(block, 1), :]

        def step(i, carry):
            at = pl.ds(pl.multiple_of(i * 32, 32), 32)
            v = lat[at, :].astype(F32) + use * cond[at, :].astype(F32)
            center = v - jnp.mean(v, axis=-1, keepdims=True)
            var = jnp.mean(center * center, axis=-1, keepdims=True)
            store(at, (center * lax.rsqrt(var + 1e-6) * scale + shift).astype(BF16))
            return carry

        lax.fori_loop(lo, hi, step, 0)

    def store_stage(at, v):
        xst[at, :] = v

    def store_own(at, v):
        xbuf[c, at, :] = v

    def half(h):
        return slice(None) if h is None else pl.ds(h * WROWS, WROWS)

    def view_q(zz, h):
        return wbuf.at[0, y, zz, half(h)]

    def view_b(zz, h):
        return wbuf.at[1, y, zz, half(h)]

    def view_a(zz, h):
        return wbuf.at[2, :, zz, half(h)]

    def view_o(zz, h):
        base = seq_of(y, zz, c)
        return owb.at[base] if h is None else owb.at[base, pl.ds(h * 48, 48)]

    b_y, q_y = [], []

    def forward(j, zz, kept):
        kept.append((push(wbuf.at[j, y, zz], wbuf.at[j, y, zz], row), wbuf.at[j, 1 - y, zz]))

    w_own.wait()
    arrived(wbuf.at[:, y, z, sib_rows], w_sib)
    for i, rows in zip(y_first, (own_rows, sib_rows)):
        arrived(wbuf.at[1:3, 1 - y, z, rows], i)
    got_a = ring_send(view_a, 0)
    for load in loads[2:]:
        load.wait()
    g = x * 4 + tp
    near = lat[:, pl.ds(pl.multiple_of(g * 3 // 2 * HEAD, HEAD), 2 * HEAD)].astype(F32)
    near = jnp.where(g % 2 == 0, near[:, :2 * WROWS], near[:, HEAD // 2:])
    res[...] = jnp.transpose(near)

    layer_norm(1 - c, store_stage, 0, 4)

    def q_hop(t, got):
        ring_wait(view_q, t, got)
        if t < 4:
            got = ring_send(view_q, t)
            forward(0, zm(t), q_y)
            forward(0, zp(t), q_y)
            return got
        forward(0, zp(t), q_y)

    got_b = None
    for t in range(1, 5):
        if t == 1:
            for dz, zz in ((1, zm(1)), (7, zp(1))):
                for e, rows in enumerate((own_rows, sib_rows)):
                    arrived(wbuf.at[1, y, zz, rows], k_first[dz, e])
        else:
            ring_wait(view_b, t, got_b)
        if t < 4:
            got_b = ring_send(view_b, t)
            forward(1, zm(t), b_y)
            forward(1, zp(t), b_y)
            ring_wait(view_a, t, got_a)
            got_a = ring_send(view_a, t)
            if t == 1:
                got_q = ring_send(view_q, 0)
                forward(0, z, q_y)
                layer_norm(1 - c, store_stage, 4, 8)
                x_sib = push(xst, xbuf.at[c], sib)
            else:
                got_q = q_hop(t - 1, got_q)
                layer_norm(c, store_own, 4 * t - 8, 4 * t - 4)
        else:
            forward(1, zp(t), b_y)
    arrived(xbuf.at[1 - c], x_sib)
    for i, land in b_y:
        arrived(land, i)

    def head_norm(v, g):
        return v * lax.rsqrt(jnp.mean(v * v, axis=-1, keepdims=True) + 1e-6) * g

    q_gain = gain[c, 0:1, :] * (math.log2(math.e) / math.sqrt(HEAD))
    k_gain = gain[c, 1:2, :]

    def project_in(j, store):
        def step(m, carry):
            store(m, jnp.dot(xbuf[m], wbuf[j].reshape(D, HEAD), preferred_element_type=F32))
            return carry

        lax.fori_loop(0, 2, step, 0)

    def rows_of(m):
        return pl.ds(pl.multiple_of(m * ROWS, ROWS), ROWS)

    def store_k(m, v):
        kst[m] = jnp.transpose(head_norm(v, k_gain)).astype(BF16)

    def store_v(m, v):
        vst[rows_of(m), :] = v.astype(BF16)

    def store_q(m, v):
        v = head_norm(v, q_gain).astype(BF16)
        for h in range(2):
            qst[h, m] = v[h * HEAD:(h + 1) * HEAD]

    stays = y == c
    leaves = jnp.logical_not(stays)

    def view_k(zz, h):
        return kbuf.at[c, zz] if h is None else kbuf.at[c, zz, h]

    def view_v(zz, h):
        return vbuf.at[c, zz] if h is None else vbuf.at[c, zz, pl.ds(h * ROWS, ROWS)]

    def first_hop(staged, buf):
        i_diag, i_ring = next(ids), (next(ids), next(ids))
        diag_copy = remote(staged, buf.at[y, z], diag, i_diag)
        mine = buf.at[c, z]
        ring = [remote(mine, mine, device, i) for device, i in zip((right, left), i_ring)]
        sent.extend(ring)

        @pl.when(stays)
        def _():
            buf[y, z] = staged[...]
            for copy in ring:
                copy.start()

        @pl.when(leaves)
        def _():
            diag_copy.start()

        def late():
            @pl.when(leaves)
            def _():
                arrived(mine, i_diag)
                for copy in ring:
                    copy.start()

        return i_ring, diag_copy, late

    project_in(1, store_k)
    got_k, k_diag, late = first_hop(kst, kbuf)
    got_q = q_hop(3, got_q)
    ring_wait(view_a, 4, got_a)
    late_k = late

    @pl.when(moves)
    def _():
        ow_copy.wait_send()
        arrived(owb.at[s], ow_id)

    o_y, o_s = [], []

    def o_pass(zz):
        here, there = owb.at[seq_of(y, zz, c)], owb.at[seq_of(1 - y, zz, c)]
        o_y.append((push(here, here, row), there))
        o_s.append((push(here, here, sib), owb.at[seq_of(y, zz, 1 - c)]))

    def o_hop(t, got):
        ring_wait(view_o, t, got)
        if t < 4:
            got = ring_send(view_o, t)
            o_pass(zm(t))
            o_pass(zp(t))
            return got
        o_pass(zp(t))

    got_o = ring_send(view_o, 0)
    o_pass(z)
    project_in(2, store_v)
    got_v, v_diag, late = first_hop(vst, vbuf)
    late_k()
    late()

    shared = {}

    def share(buf, zz, t):
        mine = buf.at[c, zz]
        shared.setdefault(t, []).append((push(mine, mine, sib), buf.at[1 - c, zz]))

    share(kbuf, z, 0)
    share(vbuf, z, 0)
    def k_hop(t, got):
        ring_wait(view_k, t, got)
        if t < 4:
            got = ring_send(view_k, t)
            share(kbuf, zm(t), t)
        share(kbuf, zp(t), t)
        return got

    def v_hop(t, got):
        ring_wait(view_v, t, got)
        if t < 4:
            got = ring_send(view_v, t)
            share(vbuf, zm(t), t)
        share(vbuf, zp(t), t)
        return got

    got_k = k_hop(1, got_k)
    q_hop(4, got_q)
    acc[...] = jnp.zeros_like(acc)
    ones = jnp.ones((CHIP, HEAD), BF16)
    for i, land in q_y:
        arrived(land, i)
    got_v = v_hop(1, got_v)
    project_in(0, store_q)
    q_id = next(ids)
    q_diag = remote(qst, qbuf, diag, q_id)

    @pl.when(stays)
    def _():
        qbuf[...] = qst[...]

    @pl.when(leaves)
    def _():
        q_diag.start()

    def attend(places, halves=(0, 2)):
        lo, hi = halves
        at = slice(lo * ROWS, hi * ROWS)
        queries = qbuf[lo:hi].reshape((hi - lo) * ROWS, HEAD)
        weights = jnp.concatenate([
            jnp.exp2(jnp.dot(queries, kbuf[r, zz, h], preferred_element_type=F32)).astype(BF16)
            for r, zz in places for h in range(2)
        ], axis=1)
        values = jnp.concatenate([
            jnp.concatenate([vbuf[r, zz], ones], axis=1) for r, zz in places
        ], axis=0)
        acc[at, :] += jnp.dot(weights, values, preferred_element_type=F32)

    def shared_come(t):
        for i, land in shared[t]:
            arrived(land, i)

    for t in range(1, 5):
        if t > 1:
            got_k = k_hop(t, got_k)
            got_v = v_hop(t, got_v)
        got_o = o_hop(t, got_o)
        if t == 1:
            @pl.when(leaves)
            def _():
                arrived(qbuf, q_id)

            attend([(c, z), (c, zm(1)), (c, zp(1))])
        if t == 2:
            attend([(c, zm(2)), (c, zp(2))])
            shared_come(0)
            attend([(1 - c, z)])
        if t == 3:
            attend([(c, zm(3)), (c, zp(3))])
            for back in (1, 2):
                shared_come(back)
                attend([(1 - c, zm(back)), (1 - c, zp(back))])
    attend([(c, zp(4))])
    shared_come(3)
    shared_come(4)

    def attend_last(h):
        attend([(1 - c, zm(3)), (1 - c, zp(3)), (1 - c, zp(4))], (h, h + 1))

    a_ids, a_copies = [], {}
    for h in range(2):
        attend_last(h)
        i0 = next(ids)
        next(ids)
        a_ids.append(i0)
        for m in range(2):
            lo = h * ROWS + m * HEAD
            part = acc[lo:lo + HEAD, :]
            ast[h, m] = jnp.transpose(part[:, :HEAD] / part[:, HEAD:]).astype(BF16)
            copy = pltpu.make_async_remote_copy(
                src_ref=ast.at[h, m], dst_ref=abuf.at[h, x, y],
                send_sem=send_sems.at[i0 + m], recv_sem=recv_sems.at[i0 + y],
                device_id={"seq": seq_of(c, z, m)}, device_id_type=MESH,
            )
            is_self = jnp.logical_and(stays, c == m)
            a_copies[h, m] = copy, jnp.logical_not(is_self)

            @pl.when(is_self)
            def _():
                abuf[h, x, y] = ast[h, m]

            @pl.when(jnp.logical_not(is_self))
            def _():
                copy.start()

    x_ids = {}
    for h in range(2):
        for k, b in enumerate((y, 1 - y)):
            mine = abuf.at[h, x, b]
            if k:
                arrived(mine, a_ids[h] + b)
            else:
                @pl.when(leaves)
                def _():
                    arrived(mine, a_ids[h] + b)
            for d in (2, 1, 3):
                x_ids[h, k, d] = push(mine, mine, {"grp": (x + d) % 4})

    for i, land in o_y:
        arrived(land, i)
    for zz in range(Z):
        here = owb.at[seq_of(1 - y, zz, c)]
        o_s.append((push(here, here, sib), owb.at[seq_of(1 - y, zz, 1 - c)]))
    for i, land in o_s:
        arrived(land, i)

    def project(h, yh):
        total = None
        for xx in range(4):
            w = owb[pl.ds(xx * 8 + yh * 2, 2)].reshape(2 * WROWS, 2 * HEAD)
            a = abuf[h, xx].reshape(2 * HEAD, HEAD)
            term = jnp.dot(w, a, preferred_element_type=F32)
            total = term if total is None else total + term
        return total

    r_ids, totals = {}, []
    for h in range(2):
        for d in (1, 3, 2):
            for k, b in enumerate((y, 1 - y)):
                arrived(abuf.at[h, (x + 4 - d) % 4, b], x_ids[h, k, d])
        r_ids[h] = [next(ids) for _ in range(3)][0] - 1

        def piece(h, d):
            return remote(pst.at[h, d], rbuf.at[h, d], {"tp": (tp + d) % 4}, r_ids[h] + d)

        def step(i, carry):
            d = 1 + (i + 1) % 3
            pst[h, d] = project(h, (tp + d) % 4).astype(BF16)
            piece(h, d).start()
            return carry

        lax.fori_loop(0, 3, step, 0)
        totals.append(project(h, tp))

    for h in range(2):
        total = totals[h]
        for d in (1, 3, 2):
            arrived(rbuf.at[h, d], r_ids[h] + d)
            total = total + rbuf[h, d].astype(F32)
        at = slice(h * HEAD, (h + 1) * HEAD)
        out[:, at] = res[:, at] + total

    for copy in sent:
        copy.wait_send()
    for h in range(2):
        for d in range(1, 4):
            piece(h, d).wait_send()

    @pl.when(leaves)
    def _():
        for copy in (k_diag, v_diag, q_diag):
            copy.wait_send()

    for copy, remote_target in a_copies.values():
        @pl.when(remote_target)
        def _():
            copy.wait_send()


def body(latent, condition, modulation, qk_gain, qkv_weight, out_weight):
    modulation = jnp.transpose(modulation, (1, 0, 2))
    vm = pl.BlockSpec(memory_space=pltpu.VMEM)
    hbm = pl.BlockSpec(memory_space=pltpu.HBM)
    mixed = pl.pallas_call(
        kernel,
        out_shape=jax.ShapeDtypeStruct((2 * WROWS, ROWS), F32),
        in_specs=[hbm, hbm, hbm, vm, hbm, hbm],
        out_specs=vm,
        scratch_shapes=[
            pltpu.VMEM((ROWS, D), BF16),
            pltpu.VMEM((ROWS, D), BF16),
            pltpu.VMEM((3, 2, D), F32),
            pltpu.VMEM((2, WROWS, HEAD), BF16),
            pltpu.VMEM((WROWS, 2 * HEAD), BF16),
            pltpu.VMEM((3, 2, Z, 2 * WROWS, HEAD), BF16),
            pltpu.VMEM((2, ROWS, D), BF16),
            pltpu.VMEM((ROWS, D), BF16),
            pltpu.VMEM((2, 2, HEAD, HEAD), BF16),
            pltpu.VMEM((2, Z, 2, HEAD, ROWS), BF16),
            pltpu.VMEM((2, Z, CHIP, HEAD), BF16),
            pltpu.VMEM((2, HEAD, ROWS), BF16),
            pltpu.VMEM((CHIP, HEAD), BF16),
            pltpu.VMEM((2, 2, HEAD, HEAD), BF16),
            pltpu.VMEM((32, WROWS, 2 * HEAD), BF16),
            pltpu.VMEM((CHIP, 2 * HEAD), F32),
            pltpu.VMEM((2, 4, 2, HEAD, HEAD), BF16),
            pltpu.VMEM((2, 2, HEAD, HEAD), BF16),
            pltpu.VMEM((2, 4, 2 * WROWS, HEAD), BF16),
            pltpu.VMEM((2, 4, 2 * WROWS, HEAD), BF16),
            pltpu.VMEM((2 * WROWS, ROWS), F32),
            pltpu.SemaphoreType.DMA((N_SEMS,)),
            pltpu.SemaphoreType.DMA((N_SEMS,)),
            pltpu.SemaphoreType.DMA((5,)),
        ],
        compiler_params=pltpu.CompilerParams(
            collective_id=0, has_side_effects=True, vmem_limit_bytes=56 * 1024 * 1024
        ),
        cost_estimate=pl.CostEstimate(
            flops=3_900_000_000, bytes_accessed=4_000_000, transcendentals=4_200_000
        ),
    )(latent, condition, modulation, qk_gain, qkv_weight, jnp.transpose(out_weight, (0, 2, 1)))
    return mixed.astype(BF16).T


def solution(mesh):
    return jax.shard_map(
        body,
        mesh=mesh,
        in_specs=(
            P("seq", None),
            P("seq", None),
            P(),
            P(),
            P(None, None, "seq", ("grp", "tp")),
            P(None, ("grp", "tp"), "seq"),
        ),
        out_specs=P("seq", ("grp", "tp")),
        check_vma=False,
    )
```

profile of v0, /device:TPU:1, one launch (start us, length us, event | category | flops | bytes accessed | tf_op | source)
XLA Modules:
  0.0 95.4 jit_solution(170758164191197497)
XLA Ops:
  0.0 93.8 %shard_map.64 = f32[192,256]{1,0:T(8,128)} custom-call(bf16[256,3072]{1,0:T(8,128)(2,1)} %lat_in.1, bf16[256,3072]{1,0:T(8,128)(2,1)} %cond_in.1, f32[3,2,3072]{2,1,0:T(2,128)} %bitcast.4, f32[2,2,128]{2,1,0:T(2,128)} %gain.1, bf16[2,3,96,128]{3,2,1,0:T(8,128)(2,1)} %wsh.1, bf16[2,96,128]{2,1,0:T(8,128)(2,1)} %bitcast.5), custom_call_target="tpu_custom_call" | custom-call | flops 3900000000 | bytes 4000000 | tf_op jit(solution)/shard_map/pallas_call | solution.py:520
  93.8 1.6 %convert_bitcast_fusion = bf16[256,192]{0,1:T(8,128)(2,1)} fusion(f32[192,256]{1,0:T(8,128)} %shard_map.64), kind=kLoop, calls=%fused_computation | loop fusion | flops 49152 | bytes 294912 | tf_op jit(solution)/shard_map/transpose | solution.py:558
where the time goes:
time: 95.7 us; the launch traced here: 95.4 us
  Pallas kernels  93.8 us (98%)
  other arithmetic  1.58 us (2%)
    pallas_call x1, Pallas kernels, body(): pl.pallas_call(kernel, out_shape=jax.ShapeDtypeStruct((2 * WROWS, ROWS),...  93.8 us

commit v1 on v0

--- a/solution.py
+++ b/solution.py
@@ -20,7 +20,7 @@
 
 def kernel(
     lat_in, cond_in, mod_in, gain, wsh, ow_in, out,
-    lat, cond, mod, ow, owt, wbuf, xbuf, xst, qbuf, kbuf, vbuf, kst, vst, qst, owb, acc, abuf, ast, pst, rbuf, res,
+    lat, cond, mod, ow, owt, wbuf, xbuf, xst, qbuf, kbuf, vbuf, owb, acc, abuf, ast, pst, rbuf, res,
     send_sems, recv_sems, load_sems,
 ):
     loads = []
@@ -35,7 +35,7 @@
 
     sib = {"seq": seq_of(y, z, 1 - c)}
     row = {"seq": seq_of(1 - y, z, c)}
-    diag = {"seq": seq_of(1 - y, z, 1 - c)}
+    beyond = {"tp": (tp + c * (3 - 2 * y)) % 4, "seq": seq_of(1 - y, z, y)}
     right = {"seq": seq_of(y, (z + 1) % Z, c)}
     left = {"seq": seq_of(y, (z + 7) % Z, c)}
 
@@ -58,9 +58,11 @@
     for i in range(1, 16):
         f = (flat + i) % 16
         greet({"grp": f // 4, "seq": seq_of((f // 2) % 2, z, f % 2)})
-    for dz in (1, 7):
-        for core in (c, 1 - c):
-            greet({"seq": seq_of(y, (z + dz) % Z, core)})
+    for device in (right, left):
+        greet(device)
+    for i in (1, 3):
+        for core in range(2):
+            greet({"tp": (tp + i) % 4, "seq": seq_of(1 - y, z, core)})
     for i in range(1, 4):
         greet({"tp": (tp + i) % 4})
 
@@ -68,7 +70,7 @@
     def _():
         greet(partner)
 
-    pl.semaphore_wait(barrier, 22 + jnp.where(moves, 1, 0))
+    pl.semaphore_wait(barrier, 24 + jnp.where(moves, 1, 0))
 
     ids = iter(range(N_SEMS))
     sent = []
@@ -104,18 +106,13 @@
             arrived(view(zm(t), 0), got[0])
             arrived(view(zp(t), 1), got[1])
 
-    own_rows = pl.ds(pl.multiple_of(c * WROWS, 32), WROWS)
-    sib_rows = pl.ds(pl.multiple_of((1 - c) * WROWS, 32), WROWS)
-    k_first, y_first = {}, []
-    for e, core in enumerate((c, 1 - c)):
-        for dz in (1, 7):
-            near_by = {"seq": seq_of(y, (z + dz) % Z, core)}
-            k_first[dz, e] = push(wsh.at[core, 1], wbuf.at[1, y, z, own_rows], near_by)
-        across = {"seq": seq_of(1 - y, z, core)}
-        y_first.append(push(wsh.at[core, 1:3], wbuf.at[1:3, y, z, own_rows], across))
-    w_sib = push(wsh.at[1 - c], wbuf.at[:, y, z, own_rows], sib)
-    w_own = pltpu.make_async_copy(wsh.at[c], wbuf.at[:, y, z, own_rows], load_sems.at[4])
-    w_own.start()
+    stays = y == c
+    leaves = jnp.logical_not(stays)
+    w_own, w_row = {}, {}
+    for j in (1, 2, 0):
+        w_row[j] = push(wsh.at[1 - y, j], wbuf.at[j, y, z, c], row)
+        w_own[j] = pltpu.make_async_copy(wsh.at[y, j], wbuf.at[j, y, z, c], load_sems.at[4 + j])
+        w_own[j].start()
 
     ow_id = next(ids)
     ow_copy = remote(owt, owb.at[seq_of(py, pz, c)], partner, ow_id)
@@ -152,151 +149,83 @@
 
         lax.fori_loop(lo, hi, step, 0)
 
-    def store_stage(at, v):
-        xst[at, :] = v
-
-    def store_own(at, v):
-        xbuf[c, at, :] = v
-
-    def half(h):
-        return slice(None) if h is None else pl.ds(h * WROWS, WROWS)
-
-    def view_q(zz, h):
-        return wbuf.at[0, y, zz, half(h)]
-
-    def view_b(zz, h):
-        return wbuf.at[1, y, zz, half(h)]
-
-    def view_a(zz, h):
-        return wbuf.at[2, :, zz, half(h)]
+    def store_to(k):
+        def store(at, v):
+            xst[k, at, :] = v
+
+        return store
+
+    def view_w(j):
+        def view(zz, h):
+            return wbuf.at[j, :, zz, c] if h is None else wbuf.at[j, :, zz, c, pl.ds(h * 48, 48)]
+
+        return view
+
+    w_shared = {0: [], 1: [], 2: []}
+
+    def w_share(j, zz):
+        mine = wbuf.at[j, :, zz, c]
+        w_shared[j].append((push(mine, mine, sib), wbuf.at[j, :, zz, 1 - c]))
+
+    def w_hop(j, t, got):
+        if t == 0:
+            w_own[j].wait()
+            arrived(wbuf.at[j, 1 - y, z, c], w_row[j])
+        else:
+            ring_wait(view_w(j), t, got)
+        if 0 < t < 4:
+            w_share(j, zm(t))
+        if t < 4:
+            got = ring_send(view_w(j), t)
+        w_share(j, zp(t))
+        return got
+
+    def w_come(j):
+        for i, land in w_shared[j]:
+            arrived(land, i)
 
     def view_o(zz, h):
         base = seq_of(y, zz, c)
         return owb.at[base] if h is None else owb.at[base, pl.ds(h * 48, 48)]
 
-    b_y, q_y = [], []
-
-    def forward(j, zz, kept):
-        kept.append((push(wbuf.at[j, y, zz], wbuf.at[j, y, zz], row), wbuf.at[j, 1 - y, zz]))
-
-    w_own.wait()
-    arrived(wbuf.at[:, y, z, sib_rows], w_sib)
-    for i, rows in zip(y_first, (own_rows, sib_rows)):
-        arrived(wbuf.at[1:3, 1 - y, z, rows], i)
-    got_a = ring_send(view_a, 0)
+    got_w = {j: w_hop(j, 0, None) for j in (1, 2, 0)}
     for load in loads[2:]:
         load.wait()
+    x_base = [next(ids) for _ in range(4)][0]
+    beyond_copies = [
+        pltpu.make_async_remote_copy(
+            src_ref=xst.at[0, pl.ds(part * HEAD, HEAD)], dst_ref=xbuf.at[c, pl.ds(part * HEAD, HEAD)],
+            send_sem=send_sems.at[x_base + part], recv_sem=recv_sems.at[x_base + 2 * part + c],
+            device_id=beyond, device_id_type=MESH,
+        )
+        for part in range(2)
+    ]
+    sent.extend(beyond_copies)
+    layer_norm(1 - y, store_to(0), 0, 4)
+    beyond_copies[0].start()
+    layer_norm(1 - y, store_to(0), 4, 8)
+    beyond_copies[1].start()
     g = x * 4 + tp
     near = lat[:, pl.ds(pl.multiple_of(g * 3 // 2 * HEAD, HEAD), 2 * HEAD)].astype(F32)
     near = jnp.where(g % 2 == 0, near[:, :2 * WROWS], near[:, HEAD // 2:])
     res[...] = jnp.transpose(near)
 
-    layer_norm(1 - c, store_stage, 0, 4)
-
-    def q_hop(t, got):
-        ring_wait(view_q, t, got)
-        if t < 4:
-            got = ring_send(view_q, t)
-            forward(0, zm(t), q_y)
-            forward(0, zp(t), q_y)
-            return got
-        forward(0, zp(t), q_y)
-
-    got_b = None
+    x_id = next(ids)
+    x_local = pltpu.make_async_copy(xst.at[1], xbuf.at[c], load_sems.at[7])
+    x_remote = remote(xst.at[1], xbuf.at[c], sib, x_id)
     for t in range(1, 5):
-        if t == 1:
-            for dz, zz in ((1, zm(1)), (7, zp(1))):
-                for e, rows in enumerate((own_rows, sib_rows)):
-                    arrived(wbuf.at[1, y, zz, rows], k_first[dz, e])
-        else:
-            ring_wait(view_b, t, got_b)
-        if t < 4:
-            got_b = ring_send(view_b, t)
-            forward(1, zm(t), b_y)
-            forward(1, zp(t), b_y)
-            ring_wait(view_a, t, got_a)
-            got_a = ring_send(view_a, t)
-            if t == 1:
-                got_q = ring_send(view_q, 0)
-                forward(0, z, q_y)
-                layer_norm(1 - c, store_stage, 4, 8)
-                x_sib = push(xst, xbuf.at[c], sib)
-            else:
-                got_q = q_hop(t - 1, got_q)
-                layer_norm(c, store_own, 4 * t - 8, 4 * t - 4)
-        else:
-            forward(1, zp(t), b_y)
-    arrived(xbuf.at[1 - c], x_sib)
-    for i, land in b_y:
-        arrived(land, i)
-
-    def head_norm(v, g):
-        return v * lax.rsqrt(jnp.mean(v * v, axis=-1, keepdims=True) + 1e-6) * g
-
-    q_gain = gain[c, 0:1, :] * (math.log2(math.e) / math.sqrt(HEAD))
-    k_gain = gain[c, 1:2, :]
-
-    def project_in(j, store):
-        def step(m, carry):
-            store(m, jnp.dot(xbuf[m], wbuf[j].reshape(D, HEAD), preferred_element_type=F32))
-            return carry
-
-        lax.fori_loop(0, 2, step, 0)
-
-    def rows_of(m):
-        return pl.ds(pl.multiple_of(m * ROWS, ROWS), ROWS)
-
-    def store_k(m, v):
-        kst[m] = jnp.transpose(head_norm(v, k_gain)).astype(BF16)
-
-    def store_v(m, v):
-        vst[rows_of(m), :] = v.astype(BF16)
-
-    def store_q(m, v):
-        v = head_norm(v, q_gain).astype(BF16)
-        for h in range(2):
-            qst[h, m] = v[h * HEAD:(h + 1) * HEAD]
-
-    stays = y == c
-    leaves = jnp.logical_not(stays)
-
-    def view_k(zz, h):
-        return kbuf.at[c, zz] if h is None else kbuf.at[c, zz, h]
-
-    def view_v(zz, h):
-        return vbuf.at[c, zz] if h is None else vbuf.at[c, zz, pl.ds(h * ROWS, ROWS)]
-
-    def first_hop(staged, buf):
-        i_diag, i_ring = next(ids), (next(ids), next(ids))
-        diag_copy = remote(staged, buf.at[y, z], diag, i_diag)
-        mine = buf.at[c, z]
-        ring = [remote(mine, mine, device, i) for device, i in zip((right, left), i_ring)]
-        sent.extend(ring)
-
-        @pl.when(stays)
-        def _():
-            buf[y, z] = staged[...]
-            for copy in ring:
-                copy.start()
-
-        @pl.when(leaves)
-        def _():
-            diag_copy.start()
-
-        def late():
+        for j in (1, 2, 0):
+            got_w[j] = w_hop(j, t, got_w[j])
+        if t < 3:
+            layer_norm(y, store_to(1), 4 * t - 4, 4 * t)
+        if t == 2:
+            @pl.when(stays)
+            def _():
+                x_local.start()
+
             @pl.when(leaves)
             def _():
-                arrived(mine, i_diag)
-                for copy in ring:
-                    copy.start()
-
-        return i_ring, diag_copy, late
-
-    project_in(1, store_k)
-    got_k, k_diag, late = first_hop(kst, kbuf)
-    got_q = q_hop(3, got_q)
-    ring_wait(view_a, 4, got_a)
-    late_k = late
+                x_remote.start()
 
     @pl.when(moves)
     def _():
@@ -321,10 +250,58 @@
 
     got_o = ring_send(view_o, 0)
     o_pass(z)
+    w_come(1)
+
+    @pl.when(stays)
+    def _():
+        x_local.wait()
+        arrived(xbuf.at[1 - c], x_id)
+
+    @pl.when(leaves)
+    def _():
+        for core in range(2):
+            for part in range(2):
+                arrived(xbuf.at[core, pl.ds(part * HEAD, HEAD)], x_base + 2 * part + core)
+
+    def head_norm(v, g):
+        return v * lax.rsqrt(jnp.mean(v * v, axis=-1, keepdims=True) + 1e-6) * g
+
+    q_gain = gain[y, 0:1, :] * (math.log2(math.e) / math.sqrt(HEAD))
+    k_gain = gain[y, 1:2, :]
+
+    def project_in(j, store):
+        def step(m, carry):
+            store(m, jnp.dot(xbuf[m], wbuf[j].reshape(D, HEAD), preferred_element_type=F32))
+            return carry
+
+        lax.fori_loop(0, 2, step, 0)
+
+    def rows_of(m):
+        return pl.ds(pl.multiple_of(m * ROWS, ROWS), ROWS)
+
+    def store_k(m, v):
+        kbuf[c, z, m] = jnp.transpose(head_norm(v, k_gain)).astype(BF16)
+
+    def store_v(m, v):
+        vbuf[c, z, rows_of(m), :] = v.astype(BF16)
+
+    def store_q(m, v):
+        v = head_norm(v, q_gain).astype(BF16)
+        for h in range(2):
+            qbuf[h, m] = v[h * HEAD:(h + 1) * HEAD]
+
+    def view_k(zz, h):
+        return kbuf.at[c, zz] if h is None else kbuf.at[c, zz, h]
+
+    def view_v(zz, h):
+        return vbuf.at[c, zz] if h is None else vbuf.at[c, zz, pl.ds(h * ROWS, ROWS)]
+
+    project_in(1, store_k)
+    got_k = ring_send(view_k, 0)
+    w_come(2)
     project_in(2, store_v)
-    got_v, v_diag, late = first_hop(vst, vbuf)
-    late_k()
-    late()
+    got_v = ring_send(view_v, 0)
+    got_o = o_hop(1, got_o)
 
     shared = {}
 
@@ -350,24 +327,10 @@
         share(vbuf, zp(t), t)
         return got
 
-    got_k = k_hop(1, got_k)
-    q_hop(4, got_q)
     acc[...] = jnp.zeros_like(acc)
     ones = jnp.ones((CHIP, HEAD), BF16)
-    for i, land in q_y:
-        arrived(land, i)
-    got_v = v_hop(1, got_v)
+    w_come(0)
     project_in(0, store_q)
-    q_id = next(ids)
-    q_diag = remote(qst, qbuf, diag, q_id)
-
-    @pl.when(stays)
-    def _():
-        qbuf[...] = qst[...]
-
-    @pl.when(leaves)
-    def _():
-        q_diag.start()
 
     def attend(places, halves=(0, 2)):
         lo, hi = halves
@@ -386,28 +349,31 @@
         for i, land in shared[t]:
             arrived(land, i)
 
+    def attend_shared(t):
+        shared_come(t)
+        attend([(1 - c, zm(t)), (1 - c, zp(t))] if t else [(1 - c, z)])
+
     for t in range(1, 5):
-        if t > 1:
-            got_k = k_hop(t, got_k)
-            got_v = v_hop(t, got_v)
-        got_o = o_hop(t, got_o)
-        if t == 1:
+        got_k = k_hop(t, got_k)
+        got_v = v_hop(t, got_v)
+        if t < 4:
+            got_o = o_hop(t + 1, got_o)
+        attend([(c, zp(4))] if t == 4 else [(c, zm(t)), (c, zp(t))] + [(c, z)] * (t == 1))
+        if t < 4:
             @pl.when(leaves)
             def _():
-                arrived(qbuf, q_id)
-
-            attend([(c, z), (c, zm(1)), (c, zp(1))])
-        if t == 2:
-            attend([(c, zm(2)), (c, zp(2))])
-            shared_come(0)
-            attend([(1 - c, z)])
-        if t == 3:
-            attend([(c, zm(3)), (c, zp(3))])
-            for back in (1, 2):
-                shared_come(back)
-                attend([(1 - c, zm(back)), (1 - c, zp(back))])
-    attend([(c, zp(4))])
-    shared_come(3)
+                attend_shared(t - 1)
+
+    @pl.when(leaves)
+    def _():
+        shared_come(3)
+
+    @pl.when(stays)
+    def _():
+        for t in range(3):
+            attend_shared(t)
+        shared_come(3)
+
     shared_come(4)
 
     def attend_last(h):
@@ -504,8 +470,7 @@
 
     @pl.when(leaves)
     def _():
-        for copy in (k_diag, v_diag, q_diag):
-            copy.wait_send()
+        x_remote.wait_send()
 
     for copy, remote_target in a_copies.values():
         @pl.when(remote_target)
@@ -528,15 +493,12 @@
             pltpu.VMEM((3, 2, D), F32),
             pltpu.VMEM((2, WROWS, HEAD), BF16),
             pltpu.VMEM((WROWS, 2 * HEAD), BF16),
-            pltpu.VMEM((3, 2, Z, 2 * WROWS, HEAD), BF16),
+            pltpu.VMEM((3, 2, Z, 2, WROWS, HEAD), BF16),
             pltpu.VMEM((2, ROWS, D), BF16),
-            pltpu.VMEM((ROWS, D), BF16),
+            pltpu.VMEM((2, ROWS, D), BF16),
             pltpu.VMEM((2, 2, HEAD, HEAD), BF16),
             pltpu.VMEM((2, Z, 2, HEAD, ROWS), BF16),
             pltpu.VMEM((2, Z, CHIP, HEAD), BF16),
-            pltpu.VMEM((2, HEAD, ROWS), BF16),
-            pltpu.VMEM((CHIP, HEAD), BF16),
-            pltpu.VMEM((2, 2, HEAD, HEAD), BF16),
             pltpu.VMEM((32, WROWS, 2 * HEAD), BF16),
             pltpu.VMEM((CHIP, 2 * HEAD), F32),
             pltpu.VMEM((2, 4, 2, HEAD, HEAD), BF16),
@@ -546,7 +508,7 @@
             pltpu.VMEM((2 * WROWS, ROWS), F32),
             pltpu.SemaphoreType.DMA((N_SEMS,)),
             pltpu.SemaphoreType.DMA((N_SEMS,)),
-            pltpu.SemaphoreType.DMA((5,)),
+            pltpu.SemaphoreType.DMA((8,)),
         ],
         compiler_params=pltpu.CompilerParams(
             collective_id=0, has_side_effects=True, vmem_limit_bytes=56 * 1024 * 1024

time: 95.7 us -> 92 us (0.961)
  Pallas kernels: 93.8 us -> 90.2 us
    pallas_call x1, Pallas kernels: 93.8 us -> 90.2 us  [body(): pl.pallas_call(kernel, out_shape=jax.ShapeDtypeStruct((2 * WROWS, ROWS),...]
where the time goes in v1:
time: 92 us; the launch traced here: 91.8 us
  Pallas kernels  90.2 us (98%)
  other arithmetic  1.58 us (2%)
    pallas_call x1, Pallas kernels, body(): pl.pallas_call(kernel, out_shape=jax.ShapeDtypeStruct((2 * WROWS, ROWS),...  90.2 us

profile of v1, /device:TPU:1, one launch (start us, length us, event | category | flops | bytes accessed | tf_op | source)
XLA Modules:
  0.0 91.8 jit_solution(16844704254017847413)
XLA Ops:
  0.0 90.2 %shard_map.64 = f32[192,256]{1,0:T(8,128)} custom-call(bf16[256,3072]{1,0:T(8,128)(2,1)} %lat_in.1, bf16[256,3072]{1,0:T(8,128)(2,1)} %cond_in.1, f32[3,2,3072]{2,1,0:T(2,128)} %bitcast.4, f32[2,2,128]{2,1,0:T(2,128)} %gain.1, bf16[2,3,96,128]{3,2,1,0:T(8,128)(2,1)} %wsh.1, bf16[2,96,128]{2,1,0:T(8,128)(2,1)} %bitcast.5), custom_call_target="tpu_custom_call" | custom-call | flops 3900000000 | bytes 4000000 | tf_op jit(solution)/shard_map/pallas_call | solution.py:485
  90.2 1.6 %convert_bitcast_fusion = bf16[256,192]{0,1:T(8,128)(2,1)} fusion(f32[192,256]{1,0:T(8,128)} %shard_map.64), kind=kLoop, calls=%fused_computation | loop fusion | flops 49152 | bytes 294912 | tf_op jit(solution)/shard_map/transpose | solution.py:520

commit v2 on v1

--- a/solution.py
+++ b/solution.py
@@ -20,7 +20,7 @@
 
 def kernel(
     lat_in, cond_in, mod_in, gain, wsh, ow_in, out,
-    lat, cond, mod, ow, owt, wbuf, xbuf, xst, qbuf, kbuf, vbuf, owb, acc, abuf, ast, pst, rbuf, res,
+    lat, cond, mod, ow, owt, wbuf, xbuf, xst, qbuf, kbuf, vbuf, owb, acc, abuf, ast, pst, rbuf, res, give, take,
     send_sems, recv_sems, load_sems,
 ):
     loads = []
@@ -280,21 +280,25 @@
         return pl.ds(pl.multiple_of(m * ROWS, ROWS), ROWS)
 
     def store_k(m, v):
-        kbuf[c, z, m] = jnp.transpose(head_norm(v, k_gain)).astype(BF16)
+        kbuf[z, m] = jnp.transpose(head_norm(v, k_gain)).astype(BF16)
 
     def store_v(m, v):
-        vbuf[c, z, rows_of(m), :] = v.astype(BF16)
+        vbuf[z, rows_of(m), :] = v.astype(BF16)
 
     def store_q(m, v):
         v = head_norm(v, q_gain).astype(BF16)
         for h in range(2):
-            qbuf[h, m] = v[h * HEAD:(h + 1) * HEAD]
+            qbuf[c, h, m] = v[h * HEAD:(h + 1) * HEAD]
 
     def view_k(zz, h):
-        return kbuf.at[c, zz] if h is None else kbuf.at[c, zz, h]
+        return kbuf.at[zz] if h is None else kbuf.at[zz, h]
 
     def view_v(zz, h):
-        return vbuf.at[c, zz] if h is None else vbuf.at[c, zz, pl.ds(h * ROWS, ROWS)]
+        return vbuf.at[zz] if h is None else vbuf.at[zz, pl.ds(h * ROWS, ROWS)]
+
+    def hop(view, t, got):
+        ring_wait(view, t, got)
+        return ring_send(view, t) if t < 4 else None
 
     project_in(1, store_k)
     got_k = ring_send(view_k, 0)
@@ -303,81 +307,54 @@
     got_v = ring_send(view_v, 0)
     got_o = o_hop(1, got_o)
 
-    shared = {}
-
-    def share(buf, zz, t):
-        mine = buf.at[c, zz]
-        shared.setdefault(t, []).append((push(mine, mine, sib), buf.at[1 - c, zz]))
-
-    share(kbuf, z, 0)
-    share(vbuf, z, 0)
-    def k_hop(t, got):
-        ring_wait(view_k, t, got)
-        if t < 4:
-            got = ring_send(view_k, t)
-            share(kbuf, zm(t), t)
-        share(kbuf, zp(t), t)
-        return got
-
-    def v_hop(t, got):
-        ring_wait(view_v, t, got)
-        if t < 4:
-            got = ring_send(view_v, t)
-            share(vbuf, zm(t), t)
-        share(vbuf, zp(t), t)
-        return got
-
     acc[...] = jnp.zeros_like(acc)
     ones = jnp.ones((CHIP, HEAD), BF16)
     w_come(0)
     project_in(0, store_q)
-
-    def attend(places, halves=(0, 2)):
+    q_id = push(qbuf.at[c], qbuf.at[c], sib)
+
+    def attend(places, r, halves=(0, 2)):
         lo, hi = halves
         at = slice(lo * ROWS, hi * ROWS)
-        queries = qbuf[lo:hi].reshape((hi - lo) * ROWS, HEAD)
+        queries = qbuf[r, lo:hi].reshape((hi - lo) * ROWS, HEAD)
         weights = jnp.concatenate([
-            jnp.exp2(jnp.dot(queries, kbuf[r, zz, h], preferred_element_type=F32)).astype(BF16)
-            for r, zz in places for h in range(2)
+            jnp.exp2(jnp.dot(queries, kbuf[zz, h], preferred_element_type=F32)).astype(BF16)
+            for zz in places for h in range(2)
         ], axis=1)
         values = jnp.concatenate([
-            jnp.concatenate([vbuf[r, zz], ones], axis=1) for r, zz in places
+            jnp.concatenate([vbuf[zz], ones], axis=1) for zz in places
         ], axis=0)
-        acc[at, :] += jnp.dot(weights, values, preferred_element_type=F32)
-
-    def shared_come(t):
-        for i, land in shared[t]:
-            arrived(land, i)
-
-    def attend_shared(t):
-        shared_come(t)
-        attend([(1 - c, zm(t)), (1 - c, zp(t))] if t else [(1 - c, z)])
+        acc[r, at, :] += jnp.dot(weights, values, preferred_element_type=F32)
 
     for t in range(1, 5):
-        got_k = k_hop(t, got_k)
-        got_v = v_hop(t, got_v)
+        got_k = hop(view_k, t, got_k)
+        got_v = hop(view_v, t, got_v)
         if t < 4:
             got_o = o_hop(t + 1, got_o)
-        attend([(c, zp(4))] if t == 4 else [(c, zm(t)), (c, zp(t))] + [(c, z)] * (t == 1))
-        if t < 4:
+            places = [zm(t), zp(t)] + [z] * (t == 1)
+            attend(places, c)
+
             @pl.when(leaves)
             def _():
-                attend_shared(t - 1)
-
-    @pl.when(leaves)
-    def _():
-        shared_come(3)
+                if t == 1:
+                    arrived(qbuf.at[1 - c], q_id)
+                attend(places, 1 - c)
 
     @pl.when(stays)
     def _():
-        for t in range(3):
-            attend_shared(t)
-        shared_come(3)
-
-    shared_come(4)
+        arrived(qbuf.at[1 - c], q_id)
+        for t in range(1, 4):
+            attend([zm(t), zp(t)] + [z] * (t == 1), 1 - c)
+
+    given = []
+    for h in range(2):
+        attend([zp(4)], 1 - c, (h, h + 1))
+        give[h] = acc[1 - c, h * ROWS:(h + 1) * ROWS, :].astype(BF16)
+        given.append(push(give.at[h], take.at[h], sib))
 
     def attend_last(h):
-        attend([(1 - c, zm(3)), (1 - c, zp(3)), (1 - c, zp(4))], (h, h + 1))
+        attend([zp(4)], c, (h, h + 1))
+        arrived(take.at[h], given[h])
 
     a_ids, a_copies = [], {}
     for h in range(2):
@@ -387,7 +364,7 @@
         a_ids.append(i0)
         for m in range(2):
             lo = h * ROWS + m * HEAD
-            part = acc[lo:lo + HEAD, :]
+            part = acc[c, lo:lo + HEAD, :] + take[h, m * HEAD:(m + 1) * HEAD, :].astype(F32)
             ast[h, m] = jnp.transpose(part[:, :HEAD] / part[:, HEAD:]).astype(BF16)
             copy = pltpu.make_async_remote_copy(
                 src_ref=ast.at[h, m], dst_ref=abuf.at[h, x, y],
@@ -496,16 +473,18 @@
             pltpu.VMEM((3, 2, Z, 2, WROWS, HEAD), BF16),
             pltpu.VMEM((2, ROWS, D), BF16),
             pltpu.VMEM((2, ROWS, D), BF16),
-            pltpu.VMEM((2, 2, HEAD, HEAD), BF16),
-            pltpu.VMEM((2, Z, 2, HEAD, ROWS), BF16),
-            pltpu.VMEM((2, Z, CHIP, HEAD), BF16),
+            pltpu.VMEM((2, 2, 2, HEAD, HEAD), BF16),
+            pltpu.VMEM((Z, 2, HEAD, ROWS), BF16),
+            pltpu.VMEM((Z, CHIP, HEAD), BF16),
             pltpu.VMEM((32, WROWS, 2 * HEAD), BF16),
-            pltpu.VMEM((CHIP, 2 * HEAD), F32),
+            pltpu.VMEM((2, CHIP, 2 * HEAD), F32),
             pltpu.VMEM((2, 4, 2, HEAD, HEAD), BF16),
             pltpu.VMEM((2, 2, HEAD, HEAD), BF16),
             pltpu.VMEM((2, 4, 2 * WROWS, HEAD), BF16),
             pltpu.VMEM((2, 4, 2 * WROWS, HEAD), BF16),
             pltpu.VMEM((2 * WROWS, ROWS), F32),
+            pltpu.VMEM((2, ROWS, 2 * HEAD), BF16),
+            pltpu.VMEM((2, ROWS, 2 * HEAD), BF16),
             pltpu.SemaphoreType.DMA((N_SEMS,)),
             pltpu.SemaphoreType.DMA((N_SEMS,)),
             pltpu.SemaphoreType.DMA((8,)),

time: 92 us -> 91.4 us (level)
  no operation moved by 1% of the time
where the time goes in v2:
time: 91.4 us; the launch traced here: 91.2 us
  Pallas kernels  89.6 us (98%)
  other arithmetic  1.58 us (2%)
    pallas_call x1, Pallas kernels, body(): pl.pallas_call(kernel, out_shape=jax.ShapeDtypeStruct((2 * WROWS, ROWS),...  89.6 us

profile of v2, /device:TPU:1, one launch (start us, length us, event | category | flops | bytes accessed | tf_op | source)
XLA Modules:
  0.0 91.2 jit_solution(17935843509143927220)
XLA Ops:
  0.0 89.6 %shard_map.64 = f32[192,256]{1,0:T(8,128)} custom-call(bf16[256,3072]{1,0:T(8,128)(2,1)} %lat_in.1, bf16[256,3072]{1,0:T(8,128)(2,1)} %cond_in.1, f32[3,2,3072]{2,1,0:T(2,128)} %bitcast.4, f32[2,2,128]{2,1,0:T(2,128)} %gain.1, bf16[2,3,96,128]{3,2,1,0:T(8,128)(2,1)} %wsh.1, bf16[2,96,128]{2,1,0:T(8,128)(2,1)} %bitcast.5), custom_call_target="tpu_custom_call" | custom-call | flops 3900000000 | bytes 4000000 | tf_op jit(solution)/shard_map/pallas_call | solution.py:462
  89.6 1.6 %convert_bitcast_fusion = bf16[256,192]{0,1:T(8,128)(2,1)} fusion(f32[192,256]{1,0:T(8,128)} %shard_map.64), kind=kLoop, calls=%fused_computation | loop fusion | flops 49152 | bytes 294912 | tf_op jit(solution)/shard_map/transpose | solution.py:499

commit v3 on v2

--- a/solution.py
+++ b/solution.py
@@ -216,6 +216,15 @@
     for t in range(1, 5):
         for j in (1, 2, 0):
             got_w[j] = w_hop(j, t, got_w[j])
+        if t == 1:
+            @pl.when(moves)
+            def _():
+                ow_copy.wait_send()
+                arrived(owb.at[s], ow_id)
+
+        else:
+            ring_wait(view_o, t - 1, got_o)
+        got_o = ring_send(view_o, t - 1)
         if t < 3:
             layer_norm(y, store_to(1), 4 * t - 4, 4 * t)
         if t == 2:
@@ -227,11 +236,6 @@
             def _():
                 x_remote.start()
 
-    @pl.when(moves)
-    def _():
-        ow_copy.wait_send()
-        arrived(owb.at[s], ow_id)
-
     o_y, o_s = [], []
 
     def o_pass(zz):
@@ -239,17 +243,6 @@
         o_y.append((push(here, here, row), there))
         o_s.append((push(here, here, sib), owb.at[seq_of(y, zz, 1 - c)]))
 
-    def o_hop(t, got):
-        ring_wait(view_o, t, got)
-        if t < 4:
-            got = ring_send(view_o, t)
-            o_pass(zm(t))
-            o_pass(zp(t))
-            return got
-        o_pass(zp(t))
-
-    got_o = ring_send(view_o, 0)
-    o_pass(z)
     w_come(1)
 
     @pl.when(stays)
@@ -305,7 +298,7 @@
     w_come(2)
     project_in(2, store_v)
     got_v = ring_send(view_v, 0)
-    got_o = o_hop(1, got_o)
+    ring_wait(view_o, 4, got_o)
 
     acc[...] = jnp.zeros_like(acc)
     ones = jnp.ones((CHIP, HEAD), BF16)
@@ -330,7 +323,8 @@
         got_k = hop(view_k, t, got_k)
         got_v = hop(view_v, t, got_v)
         if t < 4:
-            got_o = o_hop(t + 1, got_o)
+            for zz in ((z, zm(1), zp(1)), (zm(2), zp(2), zm(3)), (zp(3), zp(4)))[t - 1]:
+                o_pass(zz)
             places = [zm(t), zp(t)] + [z] * (t == 1)
             attend(places, c)
 

time: 91.4 us -> 91.1 us (level)
    pallas_call x1, Pallas kernels: 89.6 us -> 88.7 us  [body(): pl.pallas_call(kernel, out_shape=jax.ShapeDtypeStruct((2 * WROWS, ROWS),...]
where the time goes in v3:
time: 91.1 us; the launch traced here: 90.3 us
  Pallas kernels  88.7 us (97%)
  other arithmetic  1.58 us (2%)
    pallas_call x1, Pallas kernels, body(): pl.pallas_call(kernel, out_shape=jax.ShapeDtypeStruct((2 * WROWS, ROWS),...  88.7 us

profile of v3, /device:TPU:1, one launch (start us, length us, event | category | flops | bytes accessed | tf_op | source)
XLA Modules:
  0.0 90.3 jit_solution(2708493871707813252)
XLA Ops:
  0.0 88.7 %shard_map.64 = f32[192,256]{1,0:T(8,128)} custom-call(bf16[256,3072]{1,0:T(8,128)(2,1)} %lat_in.1, bf16[256,3072]{1,0:T(8,128)(2,1)} %cond_in.1, f32[3,2,3072]{2,1,0:T(2,128)} %bitcast.4, f32[2,2,128]{2,1,0:T(2,128)} %gain.1, bf16[2,3,96,128]{3,2,1,0:T(8,128)(2,1)} %wsh.1, bf16[2,96,128]{2,1,0:T(8,128)(2,1)} %bitcast.5), custom_call_target="tpu_custom_call" | custom-call | flops 3900000000 | bytes 4000000 | tf_op jit(solution)/shard_map/pallas_call | solution.py:456
  88.7 1.6 %convert_bitcast_fusion = bf16[256,192]{0,1:T(8,128)(2,1)} fusion(f32[192,256]{1,0:T(8,128)} %shard_map.64), kind=kLoop, calls=%fused_computation | loop fusion | flops 49152 | bytes 294912 | tf_op jit(solution)/shard_map/transpose | solution.py:493

commit v4 on v3

--- a/solution.py
+++ b/solution.py
@@ -15,7 +15,7 @@
 D = 3072
 HEAD = 128
 WROWS = 96
-N_SEMS = 200
+N_SEMS = 240
 
 
 def kernel(
@@ -245,16 +245,17 @@
 
     w_come(1)
 
-    @pl.when(stays)
-    def _():
-        x_local.wait()
-        arrived(xbuf.at[1 - c], x_id)
-
-    @pl.when(leaves)
-    def _():
-        for core in range(2):
-            for part in range(2):
+    def tokens_come(part):
+        @pl.when(leaves)
+        def _():
+            for core in range(2):
                 arrived(xbuf.at[core, pl.ds(part * HEAD, HEAD)], x_base + 2 * part + core)
+
+        if part == 0:
+            @pl.when(stays)
+            def _():
+                x_local.wait()
+                arrived(xbuf.at[1 - c], x_id)
 
     def head_norm(v, g):
         return v * lax.rsqrt(jnp.mean(v * v, axis=-1, keepdims=True) + 1e-6) * g
@@ -262,12 +263,9 @@
     q_gain = gain[y, 0:1, :] * (math.log2(math.e) / math.sqrt(HEAD))
     k_gain = gain[y, 1:2, :]
 
-    def project_in(j, store):
-        def step(m, carry):
-            store(m, jnp.dot(xbuf[m], wbuf[j].reshape(D, HEAD), preferred_element_type=F32))
-            return carry
-
-        lax.fori_loop(0, 2, step, 0)
+    def project_in(j, m, store):
+        rows = xbuf[:, m * HEAD:(m + 1) * HEAD, :].reshape(ROWS, D)
+        store(m, jnp.dot(rows, wbuf[j].reshape(D, HEAD), preferred_element_type=F32))
 
     def rows_of(m):
         return pl.ds(pl.multiple_of(m * ROWS, ROWS), ROWS)
@@ -280,30 +278,42 @@
 
     def store_q(m, v):
         v = head_norm(v, q_gain).astype(BF16)
-        for h in range(2):
-            qbuf[c, h, m] = v[h * HEAD:(h + 1) * HEAD]
+        for core in range(2):
+            qbuf[c, m, core] = v[core * HEAD:(core + 1) * HEAD]
 
     def view_k(zz, h):
-        return kbuf.at[zz] if h is None else kbuf.at[zz, h]
+        return kbuf.at[zz, h]
 
     def view_v(zz, h):
-        return vbuf.at[zz] if h is None else vbuf.at[zz, pl.ds(h * ROWS, ROWS)]
-
-    def hop(view, t, got):
-        ring_wait(view, t, got)
-        return ring_send(view, t) if t < 4 else None
-
-    project_in(1, store_k)
-    got_k = ring_send(view_k, 0)
-    w_come(2)
-    project_in(2, store_v)
-    got_v = ring_send(view_v, 0)
+        return vbuf.at[zz, pl.ds(h * ROWS, ROWS)]
+
+    def flow(view, h, t):
+        a, b = view(zm(t), h), view(zp(t), h)
+        return (push(a, a, right) if t < 3 or h == 0 else None,
+                push(b, b, left) if t < 3 or h == 1 else None)
+
+    def hop(view, h, t, got):
+        for i, zz in zip(got, (zm(t), zp(t))):
+            if i is not None:
+                arrived(view(zz, h), i)
+        return flow(view, h, t) if t < 4 else None
+
+    got_kv = {}
+    for part in range(2):
+        tokens_come(part)
+        project_in(1, part, store_k)
+        got_kv[part, 0] = flow(view_k, part, 0)
+        if part == 0:
+            w_come(2)
+        project_in(2, part, store_v)
+        got_kv[part, 1] = flow(view_v, part, 0)
     ring_wait(view_o, 4, got_o)
 
     acc[...] = jnp.zeros_like(acc)
     ones = jnp.ones((CHIP, HEAD), BF16)
     w_come(0)
-    project_in(0, store_q)
+    for part in range(2):
+        project_in(0, part, store_q)
     q_id = push(qbuf.at[c], qbuf.at[c], sib)
 
     def attend(places, r, halves=(0, 2)):
@@ -320,8 +330,9 @@
         acc[r, at, :] += jnp.dot(weights, values, preferred_element_type=F32)
 
     for t in range(1, 5):
-        got_k = hop(view_k, t, got_k)
-        got_v = hop(view_v, t, got_v)
+        for part in range(2):
+            for i, view in enumerate((view_k, view_v)):
+                got_kv[part, i] = hop(view, part, t, got_kv[part, i])
         if t < 4:
             for zz in ((z, zm(1), zp(1)), (zm(2), zp(2), zm(3)), (zp(3), zp(4)))[t - 1]:
                 o_pass(zz)

time: 91.1 us -> 89 us (0.977)
  Pallas kernels: 88.7 us -> 86.1 us
    pallas_call x1, Pallas kernels: 88.7 us -> 86.1 us  [body(): pl.pallas_call(kernel, out_shape=jax.ShapeDtypeStruct((2 * WROWS, ROWS),...]
where the time goes in v4:
time: 89 us; the launch traced here: 87.7 us
  Pallas kernels  86.1 us (97%)
  other arithmetic  1.58 us (2%)
    pallas_call x1, Pallas kernels, body(): pl.pallas_call(kernel, out_shape=jax.ShapeDtypeStruct((2 * WROWS, ROWS),...  86.1 us

profile of v4, /device:TPU:1, one launch (start us, length us, event | category | flops | bytes accessed | tf_op | source)
XLA Modules:
  0.0 87.7 jit_solution(7066722733803332255)
XLA Ops:
  0.0 86.1 %shard_map.64 = f32[192,256]{1,0:T(8,128)} custom-call(bf16[256,3072]{1,0:T(8,128)(2,1)} %lat_in.1, bf16[256,3072]{1,0:T(8,128)(2,1)} %cond_in.1, f32[3,2,3072]{2,1,0:T(2,128)} %bitcast.4, f32[2,2,128]{2,1,0:T(2,128)} %gain.1, bf16[2,3,96,128]{3,2,1,0:T(8,128)(2,1)} %wsh.1, bf16[2,96,128]{2,1,0:T(8,128)(2,1)} %bitcast.5), custom_call_target="tpu_custom_call" | custom-call | flops 3900000000 | bytes 4000000 | tf_op jit(solution)/shard_map/pallas_call | solution.py:467
  86.1 1.6 %convert_bitcast_fusion = bf16[256,192]{0,1:T(8,128)(2,1)} fusion(f32[192,256]{1,0:T(8,128)} %shard_map.64), kind=kLoop, calls=%fused_computation | loop fusion | flops 49152 | bytes 294912 | tf_op jit(solution)/shard_map/transpose | solution.py:504
